TPU v7x, 32 devices: a whole 2x2x4 slice. The times are simulated.
32 devices in a mesh: groups: 2 (over x), tensor: 8 (over z, y), replica: 2 (over core).
Axes of the slice: x: 2, y: 2, z: 4, core: 2. Of those that a mesh axis runs over, the one named last changes fastest.
Arguments:
- query: bfloat16 [32, 8192], P(('groups', 'replica'), 'tensor'), parts along dimension 0
- cached_key_rows: bfloat16 [32, 1024, 1024], P(('groups', 'replica', 'tensor')), parts along dimension 0
- cached_value_rows: bfloat16 [32, 1024, 1024], P(('groups', 'replica', 'tensor')), parts along dimension 0, may hold values from -6 to 6
- lengths: int32 [32], P(('groups', 'replica', 'tensor')), parts along dimension 0, may hold values from 64 to 1024, as said below
- request_adapter_index: int32 [32], P('groups'), parts along dimension 0, may hold values from 0 to 63
- output_projection_weight: bfloat16 [8192, 8192], P('tensor'), may hold values from -0.0625 to 0.0625
- adapter_down_weight: bfloat16 [128, 64, 8192], P(('groups', 'replica'), None, 'tensor'), parts along dimension 0, may hold values from -0.0625 to 0.0625
- adapter_up_weight: bfloat16 [128, 64, 8192], P(('groups', 'replica'), None, 'tensor'), parts along dimension 0, may hold values from -0.75 to 0.75
Outputs:
- attention_out: bfloat16 [32, 8192], P(('groups', 'replica'), 'tensor'), parts along dimension 0
There are 2 independent parts, one for each index of `groups`. A program takes and returns all parts, laid end to end along the dimension named above; an argument that names none is the same for every part. Nothing has to cross between parts.
Inputs may be any that keep to these rules, and one draw needn't show every extreme that they name: `lengths`: one request has 1024 live slots and one has 64.
All inputs are finite; a program needn't handle non-finite values.
Results may differ from a plain program's by a relative error of at most 0.0061.
Values may be sent and summed in bfloat16 or wider, within the bound.
A program may use at most 128 MiB of HBM per device.

v0:
```python
import jax
import jax.numpy as jnp
from jax import lax
from jax.sharding import PartitionSpec as P

KV_HEADS = 8
HEAD_DIM = 128
GROUP = 8


def attend_rows(queries, key_block, value_block, live_counts):
    row_count = queries.shape[0]
    cache_len = key_block.shape[1]
    grouped = queries.reshape(row_count, KV_HEADS, GROUP, HEAD_DIM)
    key_heads = key_block.reshape(row_count, cache_len, KV_HEADS, HEAD_DIM)
    value_heads = value_block.reshape(row_count, cache_len, KV_HEADS, HEAD_DIM)
    scores = jnp.einsum(
        "bkgd,bckd->bkgc", grouped, key_heads, preferred_element_type=jnp.float32
    ) * HEAD_DIM ** (-0.5)
    live_mask = jnp.arange(cache_len)[None, None, None, :] < live_counts[:, None, None, None]
    scores = jnp.where(live_mask, scores, -1e30)
    top_score = jnp.max(scores, axis=-1, keepdims=True)
    exp_terms = jnp.where(live_mask, jnp.exp(scores - top_score), 0.0)
    weights = (exp_terms / jnp.sum(exp_terms, axis=-1, keepdims=True)).astype(jnp.bfloat16)
    attended = jnp.einsum(
        "bkgc,bckd->bkgd", weights, value_heads, preferred_element_type=jnp.float32
    )
    return attended.reshape(row_count, -1).astype(jnp.bfloat16)


def local(
    query,
    cached_key_rows,
    cached_value_rows,
    lengths,
    request_adapter_index,
    output_projection_weight,
    adapter_down_weight,
    adapter_up_weight,
):
    full_heads = lax.all_to_all(query, "tensor", split_axis=0, concat_axis=1, tiled=True)
    attended = attend_rows(full_heads, cached_key_rows, cached_value_rows, lengths)
    head_rows = lax.all_to_all(attended, "tensor", split_axis=1, concat_axis=0, tiled=True)
    row_count = head_rows.shape[0]
    base_sum = lax.psum_scatter(
        lax.dot_general(
            output_projection_weight,
            head_rows,
            (((0,), (1,)), ((), ())),
            preferred_element_type=jnp.float32,
        ),
        "tensor",
        scatter_dimension=0,
        tiled=True,
    ).T
    down_all, up_all = (
        lax.all_gather(adapter_down_weight, "replica", axis=0, tiled=True),
        lax.all_gather(adapter_up_weight, "replica", axis=0, tiled=True),
    )
    own_ids = lax.dynamic_slice_in_dim(
        request_adapter_index, lax.axis_index("replica") * row_count, row_count
    )
    down_panels = jnp.take(down_all, own_ids, axis=0)
    up_panels = jnp.take(up_all, own_ids, axis=0)
    shrink_part = jnp.einsum(
        "bi,bri->br", head_rows, down_panels, preferred_element_type=jnp.float32
    )
    shrink = lax.psum(shrink_part, "tensor").astype(jnp.bfloat16)
    delta = jnp.einsum("br,bro->bo", shrink, up_panels, preferred_element_type=jnp.float32)
    return (base_sum + delta).astype(jnp.bfloat16)


def solution(mesh):
    return jax.shard_map(
        local,
        mesh=mesh,
        in_specs=(
            P(("groups", "replica"), "tensor"),
            P(("groups", "replica", "tensor"), None, None),
            P(("groups", "replica", "tensor"), None, None),
            P(("groups", "replica", "tensor")),
            P("groups"),
            P("tensor", None),
            P(("groups", "replica"), None, "tensor"),
            P(("groups", "replica"), None, "tensor"),
        ),
        out_specs=P(("groups", "replica"), "tensor"),
        check_vma=False,
    )
```

profile of v0, /device:TPU:0, one launch (start us, length us, event | category | flops | bytes accessed | tf_op | source)
XLA Modules:
  0.0 119.8 jit_solution(11476888177740485750)
XLA Ops:
  7.4 0.7 all-gather.3.cloned.1.call-update
  8.1 0.7 all-gather.5.cloned.1.call-update
  8.8 0.5 broadcast.53
  9.4 0.6 reduce.5
  10.0 0.6 reshape.111
  10.6 7.3 %all-to-all-start = ((bf16[8,2,512]{2,1,0:T(2,128)(2,1)}), bf16[8,2,512]{2,1,0:T(2,128)(2,1)S(1)}, u32[]{:S(2)}, u32[]{:S(2)}) async-start(bf16[8,2,512]{2,1,0:T(2,128)(2,1)} %reshape.111), calls=%async_computation | async-start | bytes 32768 | tf_op jit(solution)/shard_map/all_to_all | solution.py:41
  18.6 2.7 %copy.24 = bf16[128,8,8,128]{3,2,1,0:T(8,128)(2,1)S(1)} copy(bf16[128,8,8,128]{3,1,2,0:T(8,128)(2,1)} %bitcast.42) | data formatting | bytes 4194304
  21.5 2.0 %copy.25 = bf16[128,8,8,128]{3,2,1,0:T(8,128)(2,1)} copy(bf16[128,8,8,128]{3,1,2,0:T(8,128)(2,1)S(1)} %bitcast.43) | data formatting | bytes 4194304
  23.5 1.0 all-to-all-done
  24.6 0.7 fusion.11
  25.3 0.2 fusion.35
  25.5 2.4 %fusion.14 = bf16[8,8,128]{2,1,0:T(8,128)(2,1)S(1)} fusion(bf16[1024,8,128]{2,1,0:T(8,128)(2,1)} %bitcast.44, f32[8,8]{1,0:T(8,128)S(1)} %fusion.35, f32[8,8,1024]{2,1,0:T(8,128)S(1)} %fusion.11, pred[1024]{0:T(1024)(128)(4,1)S(1)} %iota_compare_fusion), kind=kOutput, calls=%fused_computation.13 | convolution fusion | flops 17048640 | bytes 2376960 | tf_op jit(solution)/shard_map/bkgc,bckd->bkgd/dot_general | solution.py:25
  28.0 0.7 reduce.6
  28.7 0.6 reshape.113
  29.3 4.9 %all-to-all-start.1 = ((bf16[8,2,512]{2,1,0:T(2,128)(2,1)}), bf16[8,2,512]{2,1,0:T(2,128)(2,1)S(1)}, u32[]{:S(2)}, u32[]{:S(2)}) async-start(bf16[8,2,512]{2,1,0:T(2,128)(2,1)} %reshape.113), calls=%async_computation.1 | async-start | bytes 32768 | tf_op jit(solution)/shard_map/all_to_all | solution.py:43
  34.4 6.4 %all-to-all-done.1 = bf16[8,2,512]{2,1,0:T(2,128)(2,1)S(1)} async-done(((bf16[8,2,512]{2,1,0:T(2,128)(2,1)}), bf16[8,2,512]{2,1,0:T(2,128)(2,1)S(1)}, u32[]{:S(2)}, u32[]{:S(2)}) %all-to-all-start.1) | async-done | bytes 16416 | tf_op jit(solution)/shard_map/all_to_all | solution.py:43
  40.8 11.4 %convolution_bitcast_fusion = f32[8192,8]{0,1:T(8,128)} fusion(bf16[1024,8192]{1,0:T(8,128)(2,1)} %param.15, bf16[1,8,1024]{2,0,1:T(2,128)(2,1)S(1)} %bitcast.46), kind=kOutput, calls=%fused_computation.3 | convolution fusion | flops 134217728 | bytes 17055744 | tf_op jit(solution)/shard_map/dot_general | solution.py:46
  52.2 4.0 %gather_fusion = bf16[8,64,1024]{2,1,0:T(8,128)(2,1)S(1)} fusion(bf16[64,64,1024]{2,1,0:T(8,128)(2,1)} %all-gather.3.cloned.1.call-done, s32[1024]{0:T(1024)S(1)} %pad_clamp_fusion), kind=kCustom, calls=%fused_computation.clone | custom fusion | bytes 2097184 | tf_op jit(solution)/shard_map/jit(_take)/gather | solution.py:63
  56.3 4.0 %gather_fusion.1 = bf16[8,64,1024]{2,1,0:T(8,128)(2,1)S(1)} fusion(bf16[64,64,1024]{2,1,0:T(8,128)(2,1)} %all-gather.5.cloned.1.call-done, s32[1024]{0:T(1024)S(1)} %pad_clamp_fusion), kind=kCustom, calls=%fused_computation.1.clone | custom fusion | bytes 2097184 | tf_op jit(solution)/shard_map/jit(_take)/gather | solution.py:64
  60.3 0.4 fusion.19
  60.7 20.3 %psum.7 = bf16[8,64]{1,0:T(8,128)(2,1)S(1)} all-reduce(f32[8,64]{1,0:T(8,128)S(1)} %bitcast.49), channel_id=1, replica_groups=mesh['groups'=2,'tensor'=8,'replica'=2] {'tensor'}, use_global_device_ids=true, to_apply=%region_3.5 | all-reduce | flops 512 | bytes 3072 | tf_op jit(solution)/shard_map/psum | solution.py:68
  81.0 0.3 fusion.17
  81.4 29.6 %reduce-scatter.2.cloned.1.call-done = f32[1024,8]{0,1:T(8,128)} async-done(((f32[8192,8]{0,1:T(8,128)}), f32[1024,8]{0,1:T(8,128)}) %reduce-scatter.2.cloned.1.call-update) | async-done | bytes 32784 | tf_op jit(solution)/shard_map/reduce_scatter | solution.py:45
  111.0 1.4 %fusion.26 = bf16[8,1024]{1,0:T(8,128)(2,1)} fusion(f32[1024,8]{0,1:T(8,128)} %reduce-scatter.2.cloned.1.call-done, f32[8,1,1024]{2,1,0:T(1,128)S(1)} %fusion.17), kind=kLoop, calls=%fused_computation.25 | loop fusion | flops 16384 | bytes 81920 | tf_op jit(solution)/shard_map/convert_element_type | solution.py:70
  (19 shorter events, 0.6 us)
Async XLA Ops:
  7.4 44.9 %all-gather.3.cloned.1.call-start = ((), (), s32[]{:S(2)}) async-start(), calls=%async_computation.4 | async-start | bytes 12582912 | tf_op jit(solution)/shard_map/all_gather | solution.py:57
  8.1 1.3 %copy-start.1 = (bf16[8,1024]{1,0:T(8,128)(2,1)S(1)}, bf16[8,1024]{1,0:T(8,128)(2,1)}, u32[]{:S(2)}) copy-start(bf16[8,1024]{1,0:T(8,128)(2,1)} %param.10) | copy-start | bytes 49156
  8.1 48.2 %all-gather.5.cloned.1.call-start = ((), (), s32[]{:S(2)}) async-start(), calls=%async_computation.5 | async-start | bytes 12582912 | tf_op jit(solution)/shard_map/all_gather | solution.py:58
  10.6 13.9 %all-to-all-start = ((bf16[8,2,512]{2,1,0:T(2,128)(2,1)}), bf16[8,2,512]{2,1,0:T(2,128)(2,1)S(1)}, u32[]{:S(2)}, u32[]{:S(2)}) async-start(bf16[8,2,512]{2,1,0:T(2,128)(2,1)} %reshape.111), calls=%async_computation | async-start | bytes 32768 | tf_op jit(solution)/shard_map/all_to_all | solution.py:41
  18.6 2.9 %copy-start = (bf16[1,1024,1024]{2,1,0:T(8,128)(2,1)S(1)}, bf16[1,1024,1024]{2,1,0:T(8,128)(2,1)}, u32[]{:S(2)}) copy-start(bf16[1,1024,1024]{2,1,0:T(8,128)(2,1)} %param.12) | copy-start | bytes 6291460
  25.3 9.0 %copy-start.2 = (s32[16]{0:T(128)S(1)}, s32[16]{0:T(128)}, u32[]{:S(2)}) copy-start(s32[16]{0:T(128)} %param.14) | copy-start | bytes 196
  29.3 11.5 %all-to-all-start.1 = ((bf16[8,2,512]{2,1,0:T(2,128)(2,1)}), bf16[8,2,512]{2,1,0:T(2,128)(2,1)S(1)}, u32[]{:S(2)}, u32[]{:S(2)}) async-start(bf16[8,2,512]{2,1,0:T(2,128)(2,1)} %reshape.113), calls=%async_computation.1 | async-start | bytes 32768 | tf_op jit(solution)/shard_map/all_to_all | solution.py:43
  34.2 76.8 %reduce-scatter.2.cloned.1.call-start = ((), (), s32[]{:S(2)}) async-start(), calls=%async_computation.3 | async-start | bytes 294912 | tf_op jit(solution)/shard_map/reduce_scatter | solution.py:45
Sparse Core Ops, SparseCore 0:
  9.7 22.5 all-gather.2
  33.9 21.0 all-gather.4
Sparse Core Ops, SparseCore 1:
  52.3 58.7 reduce-scatter.1
where the time goes:
time: 120 us
  waiting for transfers between devices  38.5 us (32%)
  blocking collectives  20.3 us (17%)
  between operations  15.6 us (13%)
  matrix products  15.2 us (13%)
  local copies, waits for them, and re-layouts  14.7 us (12%)
  starting transfers between devices  12.3 us (10%)
  other arithmetic  3.09 us (3%)
    reduce_scatter x1, waiting for transfers between devices, local(): lax.psum_scatter(lax.dot_general(output_projection_weight, head_rows, (((...  29.6 us
    psum x1, blocking collectives, local(): shrink = lax.psum(shrink_part, 'tensor').astype(jnp.bfloat16)  20.3 us
    dot_general x1, matrix products, local(): lax.dot_general(output_projection_weight, head_rows, (((0,), (1,)), ((),...  11.4 us
    all_to_all x1, starting transfers between devices, local(): lax.all_to_all(query, 'tensor', split_axis=0, concat_axis=1, tiled=True)  7.28 us
    all_to_all x1, waiting for transfers between devices, local(): lax.all_to_all(attended, 'tensor', split_axis=1, concat_axis=0, tiled=True)  6.43 us
    unnamed x12, local copies, waits for them, and re-layouts  6.13 us
    all_to_all x1, starting transfers between devices, local(): lax.all_to_all(attended, 'tensor', split_axis=1, concat_axis=0, tiled=True)  4.92 us
    gather x1, local copies, waits for them, and re-layouts, local(): up_panels = jnp.take(up_all, own_ids, axis=0)  4.01 us
  transfers between devices with their start and end apart: 5, of which 3 were waited for; matrix products, arithmetic and copies ran while one was open for 26% of the time, Pallas kernels for 0%

commit v1 on v0

v1 whole, which is shorter than its diff:
```python
import functools

import jax
import jax.numpy as jnp
from jax import lax
from jax.experimental import pallas as pl
from jax.experimental.pallas import tpu as pltpu
from jax.sharding import PartitionSpec as P

KV_HEADS = 8
HEAD_DIM = 128
GROUP = 8
MESH = pl.DeviceIdType.MESH
NT = (((1,), (1,)), ((), ()))
NN = (((1,), (0,)), ((), ()))


def kernel(
    T, RP, R, F, NB, RANK, AL, C,
    q_hbm, k_hbm, v_hbm, len_ref, idx_ref, w_hbm, dn_hbm, up_hbm, out_ref,
    q_v, k_v, v_v, w_v, dn_v, up_v,
    q_send, q_recv, a_send, a_recv, e_buf, p_send, p_recv, d_buf, d_recv,
    loc_sem, w_sem,
    qs_sem, qr_sem, as_sem, ar_sem, es_sem, er_sem, ps_sem, pr_sem, ds_sem, dr_sem,
):
    t = lax.axis_index("tensor")
    r = lax.axis_index("replica")
    N = T * RP
    me = r * T + t
    H = F // RP
    HL = F // HEAD_DIM
    FOLD = max(1, 16 // R)
    PACK = 256 // RANK

    q_cp = pltpu.make_async_copy(q_hbm, q_v, loc_sem.at[0])
    k_cp = pltpu.make_async_copy(k_hbm.at[0], k_v, loc_sem.at[1])
    v_cp = pltpu.make_async_copy(v_hbm.at[0], v_v, loc_sem.at[2])
    dn_cp = pltpu.make_async_copy(dn_hbm, dn_v, loc_sem.at[3])
    up_cp = pltpu.make_async_copy(up_hbm, up_v, loc_sem.at[4])

    def w_cp(tt):
        cols = pl.ds(pl.multiple_of(tt * F + r * H, 128), H)
        return pltpu.make_async_copy(w_hbm.at[:, cols], w_v.at[tt], w_sem.at[tt])

    q_cp.start()
    barrier = pltpu.get_barrier_semaphore()

    @pl.loop(1, N)
    def _(i):
        p = lax.rem(me + i, N)
        pl.semaphore_signal(
            barrier, inc=1,
            device_id={"tensor": lax.rem(p, T), "replica": lax.div(p, T)},
            device_id_type=MESH,
        )

    k_cp.start()
    v_cp.start()
    dn_cp.start()

    @pl.loop(1, T + 1)
    def _(i):
        w_cp(lax.rem(t + i, T)).start()

    up_cp.start()

    q_cp.wait()
    q_all = q_v[...].astype(jnp.float32)
    for h in range(HL):
        q_send[:, h, :] = q_all[:, h * HEAD_DIM:(h + 1) * HEAD_DIM]

    pl.semaphore_wait(barrier, N - 1)

    def q_rc(dst, src):
        return pltpu.make_async_remote_copy(
            src_ref=q_send.at[dst], dst_ref=q_recv.at[src],
            send_sem=qs_sem.at[dst], recv_sem=qr_sem.at[src],
            device_id={"tensor": dst}, device_id_type=MESH,
        )

    @pl.loop(1, T)
    def _(i):
        q_rc(lax.rem(t + i, T), t).start()

    q_recv[t] = q_send[t]
    k_cp.wait()

    @pl.loop(1, T)
    def _(i):
        q_rc(t, lax.rem(t + i, T)).wait_recv()

    n_per = T // KV_HEADS if T > KV_HEADS else 1
    live = len_ref[0]
    live_mask = lax.broadcasted_iota(jnp.int32, (2 * GROUP, C), 1) < live
    zero = jnp.zeros((GROUP, HEAD_DIM), jnp.float32)

    def heads_of(kv):
        if HL >= GROUP:
            per = HL // GROUP
            rows = q_recv[kv // per]
            return rows[(kv % per) * GROUP:(kv % per + 1) * GROUP]
        return jnp.concatenate([q_recv[kv * n_per + i] for i in range(n_per)], axis=0)

    weights = []
    for p in range(KV_HEADS // 2):
        pair = jnp.concatenate(
            [
                jnp.concatenate([heads_of(2 * p), zero], axis=1),
                jnp.concatenate([zero, heads_of(2 * p + 1)], axis=1),
            ],
            axis=0,
        ).astype(jnp.bfloat16)
        cols = slice(p * 2 * HEAD_DIM, (p + 1) * 2 * HEAD_DIM)
        s = lax.dot_general(pair, k_v[:, cols], NT, preferred_element_type=jnp.float32)
        s = jnp.where(live_mask, s * HEAD_DIM ** (-0.5), -1e30)
        top = jnp.max(s, axis=1, keepdims=True)
        e = jnp.where(live_mask, jnp.exp(s - top), 0.0)
        weights.append((e / jnp.sum(e, axis=1, keepdims=True)).astype(jnp.bfloat16))

    v_cp.wait()
    for p in range(KV_HEADS // 2):
        cols = slice(p * 2 * HEAD_DIM, (p + 1) * 2 * HEAD_DIM)
        o = lax.dot_general(weights[p], v_v[:, cols], NN, preferred_element_type=jnp.float32)
        o = o.astype(jnp.bfloat16).astype(jnp.float32)
        for half in range(2):
            kv = 2 * p + half
            rows = o[half * GROUP:(half + 1) * GROUP, half * HEAD_DIM:(half + 1) * HEAD_DIM]
            if HL >= GROUP:
                per = HL // GROUP
                a_send[kv // per, (kv % per) * GROUP:(kv % per + 1) * GROUP, :] = rows
            else:
                for i in range(n_per):
                    a_send[kv * n_per + i] = rows[i * HL:(i + 1) * HL]

    def a_rc(dst, src):
        return pltpu.make_async_remote_copy(
            src_ref=a_send.at[lax.rem(dst, T)], dst_ref=a_recv.at[src],
            send_sem=as_sem.at[dst], recv_sem=ar_sem.at[src],
            device_id={"tensor": lax.rem(dst, T), "replica": lax.div(dst, T)},
            device_id_type=MESH,
        )

    @pl.loop(1, N)
    def _(i):
        a_rc(lax.rem(me + i, N), me).start()

    a_recv[me] = a_send[t]
    dn_cp.wait()

    @pl.loop(1, N)
    def _(i):
        a_rc(me, lax.rem(me + i, N)).wait_recv()

    rows = jnp.concatenate(
        [a_recv[:, h, :] for h in range(HL)], axis=1
    ).astype(jnp.bfloat16)

    ids = [idx_ref[b] - r * AL for b in range(NB)]
    row2 = lax.broadcasted_iota(jnp.int32, (NB, 128), 0)
    here = jnp.zeros((NB, 128), jnp.int32)
    for b in range(NB):
        ok = jnp.where((ids[b] >= 0) & (ids[b] < AL), 1, 0)
        here = jnp.where(row2 == b, ok, here)
    local = [jnp.clip(i, 0, AL - 1) for i in ids]
    rowp = lax.broadcasted_iota(jnp.int32, (NB, 256), 0)
    slot = lax.broadcasted_iota(jnp.int32, (NB, 256), 1) // RANK
    part = jnp.zeros((NB, 256), jnp.float32)
    for j in range(NB // PACK):
        panels = jnp.concatenate([dn_v[local[j * PACK + b]] for b in range(PACK)], axis=0)
        o = lax.dot_general(rows, panels, NT, preferred_element_type=jnp.float32)
        part = jnp.where(rowp == j * PACK + slot, o, part)
    e_buf[t] = jnp.where(here > 0, part[:, :128] + part[:, 128:], 0.0)

    def e_rc(dst, src):
        return pltpu.make_async_remote_copy(
            src_ref=e_buf.at[src], dst_ref=e_buf.at[src],
            send_sem=es_sem.at[dst], recv_sem=er_sem.at[src],
            device_id={"tensor": dst}, device_id_type=MESH,
        )

    @pl.loop(1, T)
    def _(i):
        e_rc(lax.rem(t + i, T), t).start()

    def p_rc(dst, src):
        return pltpu.make_async_remote_copy(
            src_ref=p_send.at[dst], dst_ref=p_recv.at[src],
            send_sem=ps_sem.at[dst], recv_sem=pr_sem.at[src],
            device_id={"tensor": lax.rem(dst, T), "replica": lax.div(dst, T)},
            device_id_type=MESH,
        )

    def project(tt):
        w_cp(tt).wait()
        acc = lax.dot_general(rows, w_v[tt], NN, preferred_element_type=jnp.float32)
        for rr in range(RP):
            block = acc[rr * R:(rr + 1) * R]
            if FOLD > 1:
                wide = H // FOLD
                block = jnp.concatenate(
                    [block[:, f * wide:(f + 1) * wide] for f in range(FOLD)], axis=0
                )
            p_send[rr * T + tt] = block.astype(jnp.bfloat16)

    @pl.loop(1, T)
    def _(i):
        tt = lax.rem(t + i, T)
        project(tt)
        for rr in range(RP):
            p_rc(rr * T + tt, me).start()

    project(t)
    other = (1 - r) * T + t
    p_rc(other, me).start()
    p_recv[me] = p_send[me]

    up_cp.wait()

    @pl.loop(1, T)
    def _(i):
        e_rc(t, lax.rem(t + i, T)).wait_recv()

    total = e_buf[0]
    for i in range(1, T):
        total = total + e_buf[i]
    total = total.astype(jnp.bfloat16).astype(jnp.float32)
    total = jnp.concatenate([total, total], axis=1)
    delta = jnp.zeros((NB, F), jnp.float32)
    for j in range(NB // PACK):
        panels = jnp.concatenate([up_v[local[j * PACK + b]] for b in range(PACK)], axis=0)
        lhs = jnp.where(rowp == j * PACK + slot, total, 0.0).astype(jnp.bfloat16)
        delta = delta + lax.dot_general(lhs, panels, NN, preferred_element_type=jnp.float32)
    for rr in range(RP):
        d_buf[rr] = delta[rr * R:(rr + 1) * R]
    d_rc = pltpu.make_async_remote_copy(
        src_ref=d_buf.at[1 - r], dst_ref=d_recv,
        send_sem=ds_sem.at[0], recv_sem=dr_sem.at[0],
        device_id={"replica": 1 - r}, device_id_type=MESH,
    )
    d_rc.start()

    @pl.loop(1, N)
    def _(i):
        p_rc(me, lax.rem(me + i, N)).wait_recv()

    d_rc.wait_recv()
    for rr in range(RP):
        base = p_recv[rr * T].astype(jnp.float32)
        for i in range(1, T):
            base = base + p_recv[rr * T + i].astype(jnp.float32)
        if FOLD > 1:
            base = jnp.concatenate([base[f * R:(f + 1) * R] for f in range(FOLD)], axis=1)
        cols = slice(rr * H, (rr + 1) * H)
        add = d_buf[r, :, cols] + d_recv[:, cols]
        out_ref[:, cols] = (base + add).astype(jnp.bfloat16)

    @pl.loop(1, T)
    def _(i):
        dst = lax.rem(t + i, T)
        q_rc(dst, t).wait_send()
        e_rc(dst, t).wait_send()

    @pl.loop(1, N)
    def _(i):
        dst = lax.rem(me + i, N)
        a_rc(dst, me).wait_send()
        p_rc(dst, me).wait_send()

    d_rc.wait_send()


def solution(mesh):
    T = mesh.shape["tensor"]
    RP = mesh.shape["replica"]

    def local(query, keys, values, lengths, index, w, dn, up):
        R, F = query.shape
        NB = index.shape[0]
        AL, RANK, _ = dn.shape
        C = keys.shape[1]
        N = T * RP
        H = F // RP
        HL = F // HEAD_DIM
        FOLD = max(1, 16 // R)
        f32, b16 = jnp.float32, jnp.bfloat16
        dma = pltpu.SemaphoreType.DMA
        anyspec = pl.BlockSpec(memory_space=pl.ANY)
        smem = pl.BlockSpec(memory_space=pltpu.SMEM)
        return pl.pallas_call(
            functools.partial(kernel, T, RP, R, F, NB, RANK, AL, C),
            out_shape=jax.ShapeDtypeStruct((R, F), b16),
            in_specs=[anyspec, anyspec, anyspec, smem, smem, anyspec, anyspec, anyspec],
            out_specs=pl.BlockSpec(memory_space=pltpu.VMEM),
            scratch_shapes=[
                pltpu.VMEM((R, F), b16),
                pltpu.VMEM(keys.shape[1:], b16),
                pltpu.VMEM(values.shape[1:], b16),
                pltpu.VMEM((T, F, H), b16),
                pltpu.VMEM(dn.shape, b16),
                pltpu.VMEM(up.shape, b16),
                pltpu.VMEM((T, HL, HEAD_DIM), f32),
                pltpu.VMEM((T, HL, HEAD_DIM), f32),
                pltpu.VMEM((T, HL, HEAD_DIM), f32),
                pltpu.VMEM((N, HL, HEAD_DIM), f32),
                pltpu.VMEM((T, NB, 128), f32),
                pltpu.VMEM((N, R * FOLD, H // FOLD), b16),
                pltpu.VMEM((N, R * FOLD, H // FOLD), b16),
                pltpu.VMEM((RP, R, F), f32),
                pltpu.VMEM((R, F), f32),
                dma((5,)),
                dma((T,)),
                dma((T,)), dma((T,)),
                dma((N,)), dma((N,)),
                dma((T,)), dma((T,)),
                dma((N,)), dma((N,)),
                dma((1,)), dma((1,)),
            ],
            compiler_params=pltpu.CompilerParams(
                collective_id=0, has_side_effects=True,
                vmem_limit_bytes=48 * 1024 * 1024,
            ),
        )(query, keys, values, lengths, index, w, dn, up)

    return jax.shard_map(
        local,
        mesh=mesh,
        in_specs=(
            P(("groups", "replica"), "tensor"),
            P(("groups", "replica", "tensor"), None, None),
            P(("groups", "replica", "tensor"), None, None),
            P(("groups", "replica", "tensor")),
            P("groups"),
            P("tensor", None),
            P(("groups", "replica"), None, "tensor"),
            P(("groups", "replica"), None, "tensor"),
        ),
        out_specs=P(("groups", "replica"), "tensor"),
        check_vma=False,
    )
```

time: 120 us -> 29.2 us (0.24)
  waiting for transfers between devices: 38.5 us -> 0 us
  Pallas kernels: 0 us -> 23.1 us
  blocking collectives: 20.3 us -> 0 us
  matrix products: 15.2 us -> 0 us
  between operations: 15.6 us -> 0.67 us
  starting transfers between devices: 12.3 us -> 0 us
  local copies, waits for them, and re-layouts: 14.7 us -> 5.15 us
  other arithmetic: 3.09 us -> 0 us
    reduce_scatter x1 -> x0, waiting for transfers between devices: 29.6 us -> none  [local(): lax.psum_scatter(lax.dot_general(output_projection_weight, head_rows, (((...]
    pallas_call x0 -> x1, Pallas kernels: none -> 23.1 us  [local(): pl.pallas_call(functools.partial(kernel, T, RP, R, F, NB, RANK, AL, C), o...]
    psum x1 -> x0, blocking collectives: 20.3 us -> none  [local(): shrink = lax.psum(shrink_part, 'tensor').astype(jnp.bfloat16)]
    dot_general x5 -> x0, matrix products: 15.2 us -> none  [the longest x1 11.4 us: local(): lax.dot_general(output_projection_weight, head_rows, (((0,), (1,)), ((),...]
    all_to_all x2 -> x0, starting transfers between devices: 12.2 us -> none  [the longest x1 7.28 us: local(): lax.all_to_all(query, 'tensor', split_axis=0, concat_axis=1, tiled=True)]
    gather x2 -> x0, local copies, waits for them, and re-layouts: 8 us -> none  [the longest x1 4.01 us: local(): up_panels = jnp.take(up_all, own_ids, axis=0)]
    all_to_all x2 -> x0, waiting for transfers between devices: 7.46 us -> none  [the longest x1 6.43 us: local(): lax.all_to_all(attended, 'tensor', split_axis=1, concat_axis=0, tiled=True)]
    unnamed x3 -> x0, waiting for transfers between devices: 1.42 us -> none
  transfers between devices with their start and end apart: 5 -> 0, of which waited for: 3 -> 0; matrix products, arithmetic and copies ran while one was open for 26% -> 0% of each run, Pallas kernels for 0% -> 0%
where the time goes in v1:
time: 29.2 us; the launch traced here: 29 us
  Pallas kernels  23.1 us (79%)
  local copies, waits for them, and re-layouts  5.15 us (18%)
  between operations  0.67 us (2%)
    pallas_call x1, Pallas kernels, local(): pl.pallas_call(functools.partial(kernel, T, RP, R, F, NB, RANK, AL, C), o...  23.1 us
    unnamed x9, local copies, waits for them, and re-layouts  5.15 us

profile of v1, /device:TPU:0, one launch (start us, length us, event | category | flops | bytes accessed | tf_op | source)
XLA Modules:
  0.0 29.0 jit_solution(9523909974296746571)
XLA Ops:
  0.7 0.0 copy-start
  0.7 1.6 %copy-done = bf16[1,1024,1024]{2,1,0:T(8,128)(2,1)S(1)} copy-done((bf16[1,1024,1024]{2,1,0:T(8,128)(2,1)S(1)}, bf16[1,1024,1024]{2,1,0:T(8,128)(2,1)}, u32[]{:S(2)}) %copy-start) | copy-done | bytes 2097176
  2.2 0.0 copy-start.1
  2.2 1.6 %copy-done.1 = bf16[1,1024,1024]{2,1,0:T(8,128)(2,1)S(1)} copy-done((bf16[1,1024,1024]{2,1,0:T(8,128)(2,1)S(1)}, bf16[1,1024,1024]{2,1,0:T(8,128)(2,1)}, u32[]{:S(2)}) %copy-start.1) | copy-done | bytes 2097176
  3.8 0.0 copy-start.2
  3.8 0.7 %copy-done.2 = bf16[8,1024]{1,0:T(8,128)(2,1)S(1)} copy-done((bf16[8,1024]{1,0:T(8,128)(2,1)S(1)}, bf16[8,1024]{1,0:T(8,128)(2,1)}, u32[]{:S(2)}) %copy-start.2) | copy-done | bytes 16408
  4.6 0.0 copy-start.3
  4.6 0.7 %copy-done.3 = s32[16]{0:T(128)S(1)} copy-done((s32[16]{0:T(128)S(1)}, s32[16]{0:T(128)}, u32[]{:S(2)}) %copy-start.3) | copy-done | bytes 88
  5.2 23.1 %shard_map.82 = bf16[8,1024]{1,0:T(8,128)(2,1)S(1)} custom-call(bf16[8,1024]{1,0:T(8,128)(2,1)S(1)} %copy-done.2, bf16[1,1024,1024]{2,1,0:T(8,128)(2,1)S(1)} %copy-done, bf16[1,1024,1024]{2,1,0:T(8,128)(2,1)S(1)} %copy-done.1, s32[1]{0:T(128)S(6)} %copy.10.len_ref, s32[16]{0:T(128)S(1)} %copy-done.3, bf16[1024,8192]{1,0:T(8,128)(2,1)} %w_hbm.1, ...), custom_call_target="tpu_custom_call" | custom-call | tf_op jit(solution)/shard_map/pallas_call | solution.py:289
  28.3 0.6 %copy.11 = bf16[8,1024]{1,0:T(8,128)(2,1)} copy(bf16[8,1024]{1,0:T(8,128)(2,1)S(1)} %shard_map.82) | data formatting | bytes 32768
Async XLA Ops:
  0.7 1.6 %copy-start = (bf16[1,1024,1024]{2,1,0:T(8,128)(2,1)S(1)}, bf16[1,1024,1024]{2,1,0:T(8,128)(2,1)}, u32[]{:S(2)}) copy-start(bf16[1,1024,1024]{2,1,0:T(8,128)(2,1)} %k_hbm.1) | copy-start | bytes 6291460
  2.2 1.6 %copy-start.1 = (bf16[1,1024,1024]{2,1,0:T(8,128)(2,1)S(1)}, bf16[1,1024,1024]{2,1,0:T(8,128)(2,1)}, u32[]{:S(2)}) copy-start(bf16[1,1024,1024]{2,1,0:T(8,128)(2,1)} %v_hbm.1) | copy-start | bytes 6291460
  3.8 0.7 %copy-start.2 = (bf16[8,1024]{1,0:T(8,128)(2,1)S(1)}, bf16[8,1024]{1,0:T(8,128)(2,1)}, u32[]{:S(2)}) copy-start(bf16[8,1024]{1,0:T(8,128)(2,1)} %q_hbm.1) | copy-start | bytes 49156
  4.6 0.7 %copy-start.3 = (s32[16]{0:T(128)S(1)}, s32[16]{0:T(128)}, u32[]{:S(2)}) copy-start(s32[16]{0:T(128)} %idx_ref.1) | copy-start | bytes 196

commit v2 on v1

--- a/solution.py
+++ b/solution.py
@@ -17,8 +17,8 @@
 
 def kernel(
     T, RP, R, F, NB, RANK, AL, C,
-    q_hbm, k_hbm, v_hbm, len_ref, idx_ref, w_hbm, dn_hbm, up_hbm, out_ref,
-    q_v, k_v, v_v, w_v, dn_v, up_v,
+    q_hbm, k_hbm, v_hbm, len_hbm, idx_hbm, w_hbm, dn_hbm, up_hbm, out_ref,
+    len_ref, idx_ref, q_v, k_v, v_v, w_v, dn_v, up_v,
     q_send, q_recv, a_send, a_recv, e_buf, p_send, p_recv, d_buf, d_recv,
     loc_sem, w_sem,
     qs_sem, qr_sem, as_sem, ar_sem, es_sem, er_sem, ps_sem, pr_sem, ds_sem, dr_sem,
@@ -32,6 +32,9 @@
     FOLD = max(1, 16 // R)
     PACK = 256 // RANK
 
+    def wrap(x):
+        return jnp.where(x >= T, x - T, x)
+
     q_cp = pltpu.make_async_copy(q_hbm, q_v, loc_sem.at[0])
     k_cp = pltpu.make_async_copy(k_hbm.at[0], k_v, loc_sem.at[1])
     v_cp = pltpu.make_async_copy(v_hbm.at[0], v_v, loc_sem.at[2])
@@ -42,17 +45,37 @@
         cols = pl.ds(pl.multiple_of(tt * F + r * H, 128), H)
         return pltpu.make_async_copy(w_hbm.at[:, cols], w_v.at[tt], w_sem.at[tt])
 
+    len_cp = pltpu.make_async_copy(len_hbm, len_ref, loc_sem.at[5])
+    idx_cp = pltpu.make_async_copy(idx_hbm, idx_ref, loc_sem.at[6])
+
+    def many(buf, count, send, recv):
+        part = buf.at[pl.ds(0, count)]
+        return pltpu.make_async_remote_copy(
+            src_ref=part, dst_ref=part, send_sem=send.at[0], recv_sem=recv.at[0],
+            device_id={"replica": 1 - r}, device_id_type=MESH,
+        )
+
+    q_all_rc = many(q_recv, T - 1, qs_sem, qr_sem)
+    a_all_rc = many(a_recv, N - 1, as_sem, ar_sem)
+    e_all_rc = many(e_buf, T - 1, es_sem, er_sem)
+    p_all_rc = many(p_recv, N - 1, ps_sem, pr_sem)
+
     q_cp.start()
+    len_cp.start()
+    idx_cp.start()
     barrier = pltpu.get_barrier_semaphore()
 
-    @pl.loop(1, N)
-    def _(i):
-        p = lax.rem(me + i, N)
+    def greet(rr, dst):
         pl.semaphore_signal(
-            barrier, inc=1,
-            device_id={"tensor": lax.rem(p, T), "replica": lax.div(p, T)},
-            device_id_type=MESH,
-        )
+            barrier, inc=1, device_id={"tensor": dst, "replica": rr}, device_id_type=MESH
+        )
+
+    @pl.loop(1, T)
+    def _(i):
+        for rr in range(RP):
+            greet(rr, wrap(t + i))
+
+    greet(1 - r, t)
 
     k_cp.start()
     v_cp.start()
@@ -60,11 +83,13 @@
 
     @pl.loop(1, T + 1)
     def _(i):
-        w_cp(lax.rem(t + i, T)).start()
+        w_cp(wrap(t + i)).start()
 
     up_cp.start()
 
     q_cp.wait()
+    len_cp.wait()
+    idx_cp.wait()
     q_all = q_v[...].astype(jnp.float32)
     for h in range(HL):
         q_send[:, h, :] = q_all[:, h * HEAD_DIM:(h + 1) * HEAD_DIM]
@@ -74,20 +99,18 @@
     def q_rc(dst, src):
         return pltpu.make_async_remote_copy(
             src_ref=q_send.at[dst], dst_ref=q_recv.at[src],
-            send_sem=qs_sem.at[dst], recv_sem=qr_sem.at[src],
+            send_sem=qs_sem.at[0], recv_sem=qr_sem.at[0],
             device_id={"tensor": dst}, device_id_type=MESH,
         )
 
     @pl.loop(1, T)
     def _(i):
-        q_rc(lax.rem(t + i, T), t).start()
+        q_rc(wrap(t + i), t).start()
 
     q_recv[t] = q_send[t]
     k_cp.wait()
 
-    @pl.loop(1, T)
-    def _(i):
-        q_rc(t, lax.rem(t + i, T)).wait_recv()
+    q_all_rc.wait_recv()
 
     n_per = T // KV_HEADS if T > KV_HEADS else 1
     live = len_ref[0]
@@ -132,24 +155,25 @@
                 for i in range(n_per):
                     a_send[kv * n_per + i] = rows[i * HL:(i + 1) * HL]
 
-    def a_rc(dst, src):
-        return pltpu.make_async_remote_copy(
-            src_ref=a_send.at[lax.rem(dst, T)], dst_ref=a_recv.at[src],
-            send_sem=as_sem.at[dst], recv_sem=ar_sem.at[src],
-            device_id={"tensor": lax.rem(dst, T), "replica": lax.div(dst, T)},
-            device_id_type=MESH,
-        )
-
-    @pl.loop(1, N)
-    def _(i):
-        a_rc(lax.rem(me + i, N), me).start()
+    def a_rc(rr, dst, src):
+        return pltpu.make_async_remote_copy(
+            src_ref=a_send.at[dst], dst_ref=a_recv.at[src],
+            send_sem=as_sem.at[0], recv_sem=ar_sem.at[0],
+            device_id={"tensor": dst, "replica": rr}, device_id_type=MESH,
+        )
+
+    a_rc(1 - r, t, me).start()
+
+    @pl.loop(1, T)
+    def _(i):
+        dst = wrap(t + T - i)
+        for rr in range(RP):
+            a_rc(rr, dst, me).start()
 
     a_recv[me] = a_send[t]
     dn_cp.wait()
 
-    @pl.loop(1, N)
-    def _(i):
-        a_rc(me, lax.rem(me + i, N)).wait_recv()
+    a_all_rc.wait_recv()
 
     rows = jnp.concatenate(
         [a_recv[:, h, :] for h in range(HL)], axis=1
@@ -174,20 +198,19 @@
     def e_rc(dst, src):
         return pltpu.make_async_remote_copy(
             src_ref=e_buf.at[src], dst_ref=e_buf.at[src],
-            send_sem=es_sem.at[dst], recv_sem=er_sem.at[src],
+            send_sem=es_sem.at[0], recv_sem=er_sem.at[0],
             device_id={"tensor": dst}, device_id_type=MESH,
         )
 
     @pl.loop(1, T)
     def _(i):
-        e_rc(lax.rem(t + i, T), t).start()
-
-    def p_rc(dst, src):
-        return pltpu.make_async_remote_copy(
-            src_ref=p_send.at[dst], dst_ref=p_recv.at[src],
-            send_sem=ps_sem.at[dst], recv_sem=pr_sem.at[src],
-            device_id={"tensor": lax.rem(dst, T), "replica": lax.div(dst, T)},
-            device_id_type=MESH,
+        e_rc(wrap(t + i), t).start()
+
+    def p_rc(rr, dst, src):
+        return pltpu.make_async_remote_copy(
+            src_ref=p_send.at[rr * T + dst], dst_ref=p_recv.at[src],
+            send_sem=ps_sem.at[0], recv_sem=pr_sem.at[0],
+            device_id={"tensor": dst, "replica": rr}, device_id_type=MESH,
         )
 
     def project(tt):
@@ -204,21 +227,18 @@
 
     @pl.loop(1, T)
     def _(i):
-        tt = lax.rem(t + i, T)
+        tt = wrap(t + i)
         project(tt)
         for rr in range(RP):
-            p_rc(rr * T + tt, me).start()
+            p_rc(rr, tt, me).start()
 
     project(t)
-    other = (1 - r) * T + t
-    p_rc(other, me).start()
+    p_rc(1 - r, t, me).start()
     p_recv[me] = p_send[me]
 
     up_cp.wait()
 
-    @pl.loop(1, T)
-    def _(i):
-        e_rc(t, lax.rem(t + i, T)).wait_recv()
+    e_all_rc.wait_recv()
 
     total = e_buf[0]
     for i in range(1, T):
@@ -239,9 +259,11 @@
     )
     d_rc.start()
 
-    @pl.loop(1, N)
-    def _(i):
-        p_rc(me, lax.rem(me + i, N)).wait_recv()
+    q_all_rc.wait_send()
+    e_all_rc.wait_send()
+    a_all_rc.wait_send()
+
+    p_all_rc.wait_recv()
 
     d_rc.wait_recv()
     for rr in range(RP):
@@ -254,17 +276,7 @@
         add = d_buf[r, :, cols] + d_recv[:, cols]
         out_ref[:, cols] = (base + add).astype(jnp.bfloat16)
 
-    @pl.loop(1, T)
-    def _(i):
-        dst = lax.rem(t + i, T)
-        q_rc(dst, t).wait_send()
-        e_rc(dst, t).wait_send()
-
-    @pl.loop(1, N)
-    def _(i):
-        dst = lax.rem(me + i, N)
-        a_rc(dst, me).wait_send()
-        p_rc(dst, me).wait_send()
+    p_all_rc.wait_send()
 
     d_rc.wait_send()
 
@@ -284,14 +296,15 @@
         FOLD = max(1, 16 // R)
         f32, b16 = jnp.float32, jnp.bfloat16
         dma = pltpu.SemaphoreType.DMA
-        anyspec = pl.BlockSpec(memory_space=pl.ANY)
-        smem = pl.BlockSpec(memory_space=pltpu.SMEM)
+        hbm = pl.BlockSpec(memory_space=pltpu.HBM)
         return pl.pallas_call(
             functools.partial(kernel, T, RP, R, F, NB, RANK, AL, C),
             out_shape=jax.ShapeDtypeStruct((R, F), b16),
-            in_specs=[anyspec, anyspec, anyspec, smem, smem, anyspec, anyspec, anyspec],
+            in_specs=[hbm] * 8,
             out_specs=pl.BlockSpec(memory_space=pltpu.VMEM),
             scratch_shapes=[
+                pltpu.SMEM(lengths.shape, jnp.int32),
+                pltpu.SMEM(index.shape, jnp.int32),
                 pltpu.VMEM((R, F), b16),
                 pltpu.VMEM(keys.shape[1:], b16),
                 pltpu.VMEM(values.shape[1:], b16),
@@ -307,17 +320,14 @@
                 pltpu.VMEM((N, R * FOLD, H // FOLD), b16),
                 pltpu.VMEM((RP, R, F), f32),
                 pltpu.VMEM((R, F), f32),
-                dma((5,)),
+                dma((7,)),
                 dma((T,)),
-                dma((T,)), dma((T,)),
-                dma((N,)), dma((N,)),
-                dma((T,)), dma((T,)),
-                dma((N,)), dma((N,)),
+                *[dma((1,)) for _ in range(8)],
                 dma((1,)), dma((1,)),
             ],
             compiler_params=pltpu.CompilerParams(
                 collective_id=0, has_side_effects=True,
-                vmem_limit_bytes=48 * 1024 * 1024,
+                vmem_limit_bytes=63 * 1024 * 1024,
             ),
         )(query, keys, values, lengths, index, w, dn, up)
 

time: 29.2 us -> 24.1 us (0.83)
  local copies, waits for them, and re-layouts: 5.15 us -> 1.32 us
  Pallas kernels: 23.1 us -> 21.7 us
    unnamed x9 -> x1, local copies, waits for them, and re-layouts: 5.15 us -> 1.32 us
    pallas_call x1, Pallas kernels: 23.1 us -> 21.7 us  [local(): pl.pallas_call(functools.partial(kernel, T, RP, R, F, NB, RANK, AL, C), o...]
where the time goes in v2:
time: 24.1 us; the launch traced here: 23.7 us
  Pallas kernels  21.7 us (90%)
  local copies, waits for them, and re-layouts  1.32 us (5%)
  between operations  0.66 us (3%)
    pallas_call x1, Pallas kernels, local(): pl.pallas_call(functools.partial(kernel, T, RP, R, F, NB, RANK, AL, C), o...  21.7 us
    unnamed x1, local copies, waits for them, and re-layouts  1.32 us

profile of v2, /device:TPU:0, one launch (start us, length us, event | category | flops | bytes accessed | tf_op | source)
XLA Modules:
  0.0 23.7 jit_solution(1428354534327934446)
XLA Ops:
  0.7 21.7 %shard_map.82 = bf16[8,1024]{1,0:T(8,128)(2,1)} custom-call(bf16[8,1024]{1,0:T(8,128)(2,1)} %q_hbm.1, bf16[1,1024,1024]{2,1,0:T(8,128)(2,1)} %k_hbm.1, bf16[1,1024,1024]{2,1,0:T(8,128)(2,1)} %v_hbm.1, s32[1]{0:T(128)S(6)} %copy.10.len_hbm, s32[16]{0:T(128)} %idx_hbm.1, bf16[1024,8192]{1,0:T(8,128)(2,1)} %w_hbm.1, bf16[32,64,1024]{2,1,0:T(8,128)(2,1)} %dn_hbm.1, ...), custom_call_target="tpu_custom_call" | custom-call | tf_op jit(solution)/shard_map/pallas_call | solution.py:300
  22.4 1.3 %copy.11 = bf16[8,1024]{1,0:T(8,128)(2,1)} copy(bf16[8,1024]{1,0:T(8,128)(2,1)} %shard_map.82) | data formatting | bytes 32768

commit v3 on v2

--- a/solution.py
+++ b/solution.py
@@ -17,8 +17,8 @@
 
 def kernel(
     T, RP, R, F, NB, RANK, AL, C,
-    q_hbm, k_hbm, v_hbm, len_hbm, idx_hbm, w_hbm, dn_hbm, up_hbm, out_ref,
-    len_ref, idx_ref, q_v, k_v, v_v, w_v, dn_v, up_v,
+    q_hbm, k_hbm, v_hbm, len_ref, idx_hbm, w_hbm, dn_hbm, up_hbm, out_ref,
+    idx_ref, q_v, k_v, v_v, w_v, dn_v, up_v,
     q_send, q_recv, a_send, a_recv, e_buf, p_send, p_recv, d_buf, d_recv,
     loc_sem, w_sem,
     qs_sem, qr_sem, as_sem, ar_sem, es_sem, er_sem, ps_sem, pr_sem, ds_sem, dr_sem,
@@ -45,8 +45,7 @@
         cols = pl.ds(pl.multiple_of(tt * F + r * H, 128), H)
         return pltpu.make_async_copy(w_hbm.at[:, cols], w_v.at[tt], w_sem.at[tt])
 
-    len_cp = pltpu.make_async_copy(len_hbm, len_ref, loc_sem.at[5])
-    idx_cp = pltpu.make_async_copy(idx_hbm, idx_ref, loc_sem.at[6])
+    idx_cp = pltpu.make_async_copy(idx_hbm, idx_ref, loc_sem.at[5])
 
     def many(buf, count, send, recv):
         part = buf.at[pl.ds(0, count)]
@@ -61,7 +60,6 @@
     p_all_rc = many(p_recv, N - 1, ps_sem, pr_sem)
 
     q_cp.start()
-    len_cp.start()
     idx_cp.start()
     barrier = pltpu.get_barrier_semaphore()
 
@@ -88,7 +86,6 @@
     up_cp.start()
 
     q_cp.wait()
-    len_cp.wait()
     idx_cp.wait()
     q_all = q_v[...].astype(jnp.float32)
     for h in range(HL):
@@ -162,13 +159,13 @@
             device_id={"tensor": dst, "replica": rr}, device_id_type=MESH,
         )
 
-    a_rc(1 - r, t, me).start()
-
     @pl.loop(1, T)
     def _(i):
         dst = wrap(t + T - i)
         for rr in range(RP):
             a_rc(rr, dst, me).start()
+
+    a_rc(1 - r, t, me).start()
 
     a_recv[me] = a_send[t]
     dn_cp.wait()
@@ -296,14 +293,14 @@
         FOLD = max(1, 16 // R)
         f32, b16 = jnp.float32, jnp.bfloat16
         dma = pltpu.SemaphoreType.DMA
+        smem = pl.BlockSpec(memory_space=pltpu.SMEM)
         hbm = pl.BlockSpec(memory_space=pltpu.HBM)
         return pl.pallas_call(
             functools.partial(kernel, T, RP, R, F, NB, RANK, AL, C),
-            out_shape=jax.ShapeDtypeStruct((R, F), b16),
-            in_specs=[hbm] * 8,
+            out_shape=pltpu.VMEM((R, F), b16),
+            in_specs=[hbm] * 3 + [smem] + [hbm] * 4,
             out_specs=pl.BlockSpec(memory_space=pltpu.VMEM),
             scratch_shapes=[
-                pltpu.SMEM(lengths.shape, jnp.int32),
                 pltpu.SMEM(index.shape, jnp.int32),
                 pltpu.VMEM((R, F), b16),
                 pltpu.VMEM(keys.shape[1:], b16),
@@ -320,7 +317,7 @@
                 pltpu.VMEM((N, R * FOLD, H // FOLD), b16),
                 pltpu.VMEM((RP, R, F), f32),
                 pltpu.VMEM((R, F), f32),
-                dma((7,)),
+                dma((6,)),
                 dma((T,)),
                 *[dma((1,)) for _ in range(8)],
                 dma((1,)), dma((1,)),

time: 24.1 us -> 22.6 us (0.938)
  local copies, waits for them, and re-layouts: 1.32 us -> 0.61 us
  Pallas kernels: 21.7 us -> 21.1 us
    unnamed x1, local copies, waits for them, and re-layouts: 1.32 us -> 0.61 us
    pallas_call x1, Pallas kernels: 21.7 us -> 21.1 us  [local(): pl.pallas_call(functools.partial(kernel, T, RP, R, F, NB, RANK, AL, C), o...]
where the time goes in v3:
time: 22.6 us; the launch traced here: 22.4 us
  Pallas kernels  21.1 us (93%)
  between operations  0.66 us (3%)
  local copies, waits for them, and re-layouts  0.61 us (3%)
    pallas_call x1, Pallas kernels, local(): pl.pallas_call(functools.partial(kernel, T, RP, R, F, NB, RANK, AL, C), o...  21.1 us
    unnamed x1, local copies, waits for them, and re-layouts  0.61 us

profile of v3, /device:TPU:0, one launch (start us, length us, event | category | flops | bytes accessed | tf_op | source)
XLA Modules:
  0.0 22.4 jit_solution(8507292608946437351)
XLA Ops:
  0.7 21.1 %shard_map.82 = bf16[8,1024]{1,0:T(8,128)(2,1)S(1)} custom-call(bf16[8,1024]{1,0:T(8,128)(2,1)} %q_hbm.1, bf16[1,1024,1024]{2,1,0:T(8,128)(2,1)} %k_hbm.1, bf16[1,1024,1024]{2,1,0:T(8,128)(2,1)} %v_hbm.1, s32[1]{0:T(128)S(6)} %copy.11.len_ref, s32[16]{0:T(128)} %idx_hbm.1, bf16[1024,8192]{1,0:T(8,128)(2,1)} %w_hbm.1, bf16[32,64,1024]{2,1,0:T(8,128)(2,1)} %dn_hbm.1, ...), custom_call_target="tpu_custom_call" | custom-call | tf_op jit(solution)/shard_map/pallas_call | solution.py:298
  21.8 0.6 %copy.10 = bf16[8,1024]{1,0:T(8,128)(2,1)} copy(bf16[8,1024]{1,0:T(8,128)(2,1)S(1)} %shard_map.82) | data formatting | bytes 32768
